TPU v7x, 128 devices: a whole 4x4x4 slice. The times are simulated.
128 devices in a mesh: row: 8 (over z, y_lo), col: 16 (over y_hi, x, core).
Axes of the slice: x: 4, y: 4 (y_hi: 2, y_lo: 2; y = y_hi * 2 + y_lo), z: 4, core: 2. Of those that a mesh axis runs over, the one named last changes fastest.
Arguments:
- hidden: bfloat16 [2048, 26624], P('col', 'row'), may hold values from -6 to 6
- weight: bfloat16 [26624, 8192], P('row', 'col'), may hold values from -0.0546875 to 0.0546875
- grad_out: bfloat16 [2048, 8192], P('row', 'col'), may hold values from -6 to 6
Outputs:
- output: bfloat16 [2048, 8192], P('row', 'col')
- grad_hidden: bfloat16 [2048, 26624], P('col', 'row')
- grad_weight: bfloat16 [26624, 8192], P('row', 'col')
All inputs are finite; a program needn't handle non-finite values.
Results may differ from a plain program's by a relative error of at most 0.019.
Values may be sent and summed in bfloat16 or wider, within the bound.
No kernel may reach another device: no remote copies, remote signals or barrier semaphores. Data moves between devices by JAX's collectives and lax.ppermute only.
A program may use at most 128 MiB of HBM per device.

v0:
```python
import jax
import jax.numpy as jnp
from jax import lax
from jax.sharding import PartitionSpec as P


def per_device(hidden, weight, grad_out):
    cotangents = lax.all_gather(grad_out, "row", axis=0, tiled=True)
    gathered = lax.all_gather(hidden, "col", axis=0, tiled=True)
    partial_out = jnp.dot(gathered, weight, preferred_element_type=jnp.float32)
    grad_weight = lax.dot_general(
        gathered, cotangents, (((0,), (0,)), ((), ())), preferred_element_type=jnp.float32
    )
    output = lax.psum_scatter(
        partial_out.astype(jnp.bfloat16), "row", scatter_dimension=0, tiled=True
    )
    part = lax.dot_general(
        cotangents, weight, (((1,), (1,)), ((), ())), preferred_element_type=jnp.float32
    )
    part = lax.optimization_barrier(part.astype(jnp.bfloat16))
    grad_hidden = lax.psum_scatter(
        part.astype(jnp.float32).astype(jnp.bfloat16), "col", scatter_dimension=0, tiled=True
    )
    return (output, grad_hidden, grad_weight.astype(jnp.bfloat16))


def solution(mesh):
    placed = (P("col", "row"), P("row", "col"), P("row", "col"))
    return jax.shard_map(
        per_device,
        mesh=mesh,
        in_specs=placed,
        out_specs=(P("row", "col"), P("col", "row"), P("row", "col")),
        check_vma=False,
    )
```

profile of v0, /device:TPU:1, one launch (start us, length us, event | category | flops | bytes accessed | tf_op | source)
XLA Modules:
  0.0 352.4 jit_solution(8082366088749023770)
XLA Ops:
  7.2 0.0 copy-start
  7.2 0.0 all-gather.5.cloned.1.call-start
  7.2 0.7 all-gather.5.cloned.1.call-update
  7.9 0.0 all-gather.3.cloned.1.call-start
  8.0 0.7 all-gather.3.cloned.1.call-update
  8.7 0.0 reduce-scatter.5.cloned.1.call-start
  8.7 56.3 %all-gather.5.cloned.1.call-done = bf16[2048,512]{1,0:T(8,128)(2,1)} async-done(((bf16[256,512]{1,0:T(8,128)(2,1)}), bf16[2048,512]{1,0:T(8,128)(2,1)}) %all-gather.5.cloned.1.call-update) | async-done | bytes 2097168 | tf_op jit(solution)/shard_map/all_gather | solution.py:8
  65.0 0.0 copy-done
  65.0 12.5 %convolution_convert_fusion = bf16[2048,3328]{1,0:T(8,128)(2,1)} fusion(bf16[2048,512]{1,0:T(8,128)(2,1)} %all-gather.5.cloned.1.call-done, bf16[3328,512]{1,0:T(8,128)(2,1)S(1)} %copy-done), kind=kOutput, calls=%fused_computation | convolution fusion | flops 6986137600 | bytes 19136512 | tf_op jit(solution)/shard_map/dot_general | solution.py:17
  77.5 0.0 reduce-scatter.5.cloned.1.call-update
  77.5 0.0 reduce-scatter.3.cloned.1.call-start
  77.6 85.4 %all-gather.3.cloned.1.call-done = bf16[2048,3328]{1,0:T(8,128)(2,1)} async-done(((bf16[128,3328]{1,0:T(8,128)(2,1)}), bf16[2048,3328]{1,0:T(8,128)(2,1)}) %all-gather.3.cloned.1.call-update) | async-done | bytes 13631504 | tf_op jit(solution)/shard_map/all_gather | solution.py:9
  162.9 11.3 %convolution_convert_fusion.2 = bf16[2048,512]{1,0:T(8,128)(2,1)} fusion(bf16[2048,3328]{1,0:T(8,128)(2,1)} %all-gather.3.cloned.1.call-done, bf16[3328,512]{1,0:T(8,128)(2,1)S(1)} %copy-done), kind=kOutput, calls=%fused_computation.2 | convolution fusion | flops 6980370432 | bytes 19136512 | tf_op jit(solution)/shard_map/dot_general | solution.py:10
  174.2 0.0 reduce-scatter.3.cloned.1.call-update
  174.2 15.8 %convolution_convert_fusion.1 = bf16[3328,512]{1,0:T(8,128)(2,1)} fusion(bf16[2048,3328]{1,0:T(8,128)(2,1)} %all-gather.3.cloned.1.call-done, bf16[2048,512]{1,0:T(8,128)(2,1)} %all-gather.5.cloned.1.call-done), kind=kOutput, calls=%fused_computation.1 | convolution fusion | flops 6981025792 | bytes 19136512 | tf_op jit(solution)/shard_map/dot_general | solution.py:11
  190.0 101.5 %reduce-scatter.5.cloned.1.call-done = bf16[128,3328]{1,0:T(8,128)(2,1)} async-done(((bf16[2048,3328]{1,0:T(8,128)(2,1)}), bf16[128,3328]{1,0:T(8,128)(2,1)}) %reduce-scatter.5.cloned.1.call-update) | async-done | bytes 851984 | tf_op jit(solution)/shard_map/reduce_scatter | solution.py:21
  291.6 54.3 %reduce-scatter.3.cloned.1.call-done = bf16[256,512]{1,0:T(8,128)(2,1)} async-done(((bf16[2048,512]{1,0:T(8,128)(2,1)}), bf16[256,512]{1,0:T(8,128)(2,1)}) %reduce-scatter.3.cloned.1.call-update) | async-done | bytes 262160 | tf_op jit(solution)/shard_map/reduce_scatter | solution.py:14
Async XLA Ops:
  7.2 57.9 %copy-start = (bf16[3328,512]{1,0:T(8,128)(2,1)S(1)}, bf16[3328,512]{1,0:T(8,128)(2,1)}, u32[]{:S(2)}) copy-start(bf16[3328,512]{1,0:T(8,128)(2,1)} %param.4) | copy-start | bytes 10223620
  7.2 57.8 %all-gather.5.cloned.1.call-start = ((), (), s32[]{:S(2)}) async-start(), calls=%async_computation.4 | async-start | bytes 2359296 | tf_op jit(solution)/shard_map/all_gather | solution.py:8
  7.9 155.0 %all-gather.3.cloned.1.call-start = ((), (), s32[]{:S(2)}) async-start(), calls=%async_computation.2 | async-start | bytes 14483456 | tf_op jit(solution)/shard_map/all_gather | solution.py:9
  8.7 282.9 %reduce-scatter.5.cloned.1.call-start = ((), (), s32[]{:S(2)}) async-start(), calls=%async_computation.5 | async-start | bytes 14483456 | tf_op jit(solution)/shard_map/reduce_scatter | solution.py:21
  77.5 268.3 %reduce-scatter.3.cloned.1.call-start = ((), (), s32[]{:S(2)}) async-start(), calls=%async_computation.3 | async-start | bytes 2359296 | tf_op jit(solution)/shard_map/reduce_scatter | solution.py:14
Sparse Core Ops, SparseCore 0:
  9.7 55.3 all-gather.4
  67.4 95.4 all-gather.2
  167.9 123.5 reduce-scatter.4
  294.4 51.3 reduce-scatter.2
where the time goes:
time: 352 us
  waiting for transfers between devices  299 us (85%)
  matrix products  39.6 us (11%)
  between operations  13.8 us (4%)
    reduce_scatter x1, waiting for transfers between devices, per_device(): lax.psum_scatter(part.astype(jnp.float32).astype(jnp.bfloat16), 'col', sc...  102 us
    all_gather x1, waiting for transfers between devices, per_device(): gathered = lax.all_gather(hidden, 'col', axis=0, tiled=True)  85.4 us
    all_gather x1, waiting for transfers between devices, per_device(): cotangents = lax.all_gather(grad_out, 'row', axis=0, tiled=True)  56.3 us
    reduce_scatter x1, waiting for transfers between devices, per_device(): lax.psum_scatter(partial_out.astype(jnp.bfloat16), 'row', scatter_dimensi...  54.3 us
    dot_general x1, matrix products, per_device(): lax.dot_general(gathered, cotangents, (((0,), (0,)), ((), ())), preferred...  15.8 us
    dot_general x1, matrix products, per_device(): lax.dot_general(cotangents, weight, (((1,), (1,)), ((), ())), preferred_e...  12.5 us
    dot_general x1, matrix products, per_device(): partial_out = jnp.dot(gathered, weight, preferred_element_type=jnp.float32)  11.3 us
  transfers between devices with their start and end apart: 4, of which 4 were waited for; matrix products, arithmetic and copies ran while one was open for 11% of the time, Pallas kernels for 0%

commit v1 on v0

--- a/solution.py
+++ b/solution.py
@@ -6,7 +6,8 @@
 
 def per_device(hidden, weight, grad_out):
     cotangents = lax.all_gather(grad_out, "row", axis=0, tiled=True)
-    gathered = lax.all_gather(hidden, "col", axis=0, tiled=True)
+    stack = jnp.stack([hidden] * lax.axis_size("col"))
+    gathered = jnp.concatenate(lax.all_to_all(stack, "col", 0, 0), axis=0)
     partial_out = jnp.dot(gathered, weight, preferred_element_type=jnp.float32)
     grad_weight = lax.dot_general(
         gathered, cotangents, (((0,), (0,)), ((), ())), preferred_element_type=jnp.float32

time: 352 us -> 409 us (1.16)
  waiting for transfers between devices: 299 us -> 341 us
  starting transfers between devices: 0.16 us -> 8.56 us
  local copies, waits for them, and re-layouts: 0.01 us -> 7.54 us
    all_to_all x0 -> x1, waiting for transfers between devices: none -> 184 us  [per_device(): gathered = jnp.concatenate(lax.all_to_all(stack, 'col', 0, 0), axis=0)]
    all_gather x1 -> x0, waiting for transfers between devices: 85.4 us -> none  [per_device(): gathered = lax.all_gather(hidden, 'col', axis=0, tiled=True)]
    all_gather x1, waiting for transfers between devices: 56.3 us -> 0.02 us  [per_device(): cotangents = lax.all_gather(grad_out, 'row', axis=0, tiled=True)]
    reduce_scatter x1, waiting for transfers between devices: 102 us -> 131 us  [per_device(): lax.psum_scatter(part.astype(jnp.float32).astype(jnp.bfloat16), 'col', sc...]
    reduce_scatter x1, waiting for transfers between devices: 54.3 us -> 25.8 us  [per_device(): lax.psum_scatter(partial_out.astype(jnp.bfloat16), 'row', scatter_dimensi...]
    all_to_all x0 -> x1, starting transfers between devices: none -> 8.45 us  [per_device(): gathered = jnp.concatenate(lax.all_to_all(stack, 'col', 0, 0), axis=0)]
    another operation x0 -> x1, local copies, waits for them, and re-layouts: none -> 7.53 us  [per_device(): stack = jnp.stack([hidden] * lax.axis_size('col'))]
  transfers between devices with their start and end apart: 4 -> 4, of which waited for: 4 -> 3; matrix products, arithmetic and copies ran while one was open for 11% -> 9% of each run, Pallas kernels for 0% -> 0%
where the time goes in v1:
time: 409 us; the launch traced here: 408 us
  waiting for transfers between devices  341 us (83%)
  matrix products  37.8 us (9%)
  between operations  13.8 us (3%)
  starting transfers between devices  8.56 us (2%)
  local copies, waits for them, and re-layouts  7.54 us (2%)
    all_to_all x1, waiting for transfers between devices, per_device(): gathered = jnp.concatenate(lax.all_to_all(stack, 'col', 0, 0), axis=0)  184 us
    reduce_scatter x1, waiting for transfers between devices, per_device(): lax.psum_scatter(part.astype(jnp.float32).astype(jnp.bfloat16), 'col', sc...  131 us
    reduce_scatter x1, waiting for transfers between devices, per_device(): lax.psum_scatter(partial_out.astype(jnp.bfloat16), 'row', scatter_dimensi...  25.8 us
    dot_general x1, matrix products, per_device(): lax.dot_general(gathered, cotangents, (((0,), (0,)), ((), ())), preferred...  14 us
    dot_general x1, matrix products, per_device(): lax.dot_general(cotangents, weight, (((1,), (1,)), ((), ())), preferred_e...  12.5 us
    dot_general x1, matrix products, per_device(): partial_out = jnp.dot(gathered, weight, preferred_element_type=jnp.float32)  11.3 us
    all_to_all x1, starting transfers between devices, per_device(): gathered = jnp.concatenate(lax.all_to_all(stack, 'col', 0, 0), axis=0)  8.45 us
  transfers between devices with their start and end apart: 4, of which 3 were waited for; matrix products, arithmetic and copies ran while one was open for 9% of the time, Pallas kernels for 0%

profile of v1, /device:TPU:1, one launch (start us, length us, event | category | flops | bytes accessed | tf_op | source)
XLA Modules:
  0.0 408.5 jit_solution(14596774663656578006)
XLA Ops:
  7.2 0.0 copy-start
  7.2 7.5 %stack.2 = bf16[16,128,3328]{2,1,0:T(8,128)(2,1)} broadcast(bf16[128,3328]{1,0:T(8,128)(2,1)} %param.3), dimensions={1,2} | broadcast | bytes 14483456 | tf_op jit(solution)/shard_map/stack | solution.py:9
  14.7 8.4 %all-to-all-start = ((bf16[16,128,3328]{2,1,0:T(8,128)(2,1)}), bf16[16,128,3328]{2,1,0:T(8,128)(2,1)}, u32[]{:S(2)}, u32[]{:S(2)}) async-start(bf16[16,128,3328]{2,1,0:T(8,128)(2,1)} %stack.2), calls=%async_computation | async-start | bytes 27262976 | tf_op jit(solution)/shard_map/all_to_all | solution.py:10
  23.2 0.0 all-gather.2.cloned.1.call-start
  23.2 0.7 all-gather.2.cloned.1.call-update
  23.9 0.0 reduce-scatter.3.cloned.1.call-start
  23.9 183.8 %all-to-all-done = bf16[16,128,3328]{2,1,0:T(8,128)(2,1)} async-done(((bf16[16,128,3328]{2,1,0:T(8,128)(2,1)}), bf16[16,128,3328]{2,1,0:T(8,128)(2,1)}, u32[]{:S(2)}, u32[]{:S(2)}) %all-to-all-start) | async-done | bytes 13631520 | tf_op jit(solution)/shard_map/all_to_all | solution.py:10
  207.7 0.0 copy-done
  207.7 11.3 %convolution_convert_fusion.2 = bf16[2048,512]{1,0:T(8,128)(2,1)} fusion(bf16[2048,3328]{1,0:T(8,128)(2,1)} %bitcast, bf16[3328,512]{1,0:T(8,128)(2,1)S(1)} %copy-done), kind=kOutput, calls=%fused_computation.2 | convolution fusion | flops 6980370432 | bytes 19136512 | tf_op jit(solution)/shard_map/dot_general | solution.py:11
  219.0 0.0 reduce-scatter.3.cloned.1.call-update
  219.0 0.0 reduce-scatter.5.cloned.1.call-start
  219.0 0.0 all-gather.2.cloned.1.call-done
  219.1 12.5 %convolution_convert_fusion = bf16[2048,3328]{1,0:T(8,128)(2,1)} fusion(bf16[2048,512]{1,0:T(8,128)(2,1)} %all-gather.2.cloned.1.call-done, bf16[3328,512]{1,0:T(8,128)(2,1)S(1)} %copy-done), kind=kOutput, calls=%fused_computation | convolution fusion | flops 6986137600 | bytes 19136512 | tf_op jit(solution)/shard_map/dot_general | solution.py:18
  231.6 0.0 reduce-scatter.5.cloned.1.call-update
  231.6 14.0 %convolution_convert_fusion.1 = bf16[3328,512]{1,0:T(8,128)(2,1)} fusion(bf16[2048,3328]{1,0:T(8,128)(2,1)} %bitcast, bf16[2048,512]{1,0:T(8,128)(2,1)} %all-gather.2.cloned.1.call-done), kind=kOutput, calls=%fused_computation.1 | convolution fusion | flops 6981025792 | bytes 19136512 | tf_op jit(solution)/shard_map/dot_general | solution.py:12
  245.6 25.8 %reduce-scatter.3.cloned.1.call-done = bf16[256,512]{1,0:T(8,128)(2,1)} async-done(((bf16[2048,512]{1,0:T(8,128)(2,1)}), bf16[256,512]{1,0:T(8,128)(2,1)}) %reduce-scatter.3.cloned.1.call-update) | async-done | bytes 262160 | tf_op jit(solution)/shard_map/reduce_scatter | solution.py:15
  271.4 130.5 %reduce-scatter.5.cloned.1.call-done = bf16[128,3328]{1,0:T(8,128)(2,1)} async-done(((bf16[2048,3328]{1,0:T(8,128)(2,1)}), bf16[128,3328]{1,0:T(8,128)(2,1)}) %reduce-scatter.5.cloned.1.call-update) | async-done | bytes 851984 | tf_op jit(solution)/shard_map/reduce_scatter | solution.py:22
Async XLA Ops:
  7.2 200.5 %copy-start = (bf16[3328,512]{1,0:T(8,128)(2,1)S(1)}, bf16[3328,512]{1,0:T(8,128)(2,1)}, u32[]{:S(2)}) copy-start(bf16[3328,512]{1,0:T(8,128)(2,1)} %param.4) | copy-start | bytes 10223620
  14.7 193.0 %all-to-all-start = ((bf16[16,128,3328]{2,1,0:T(8,128)(2,1)}), bf16[16,128,3328]{2,1,0:T(8,128)(2,1)}, u32[]{:S(2)}, u32[]{:S(2)}) async-start(bf16[16,128,3328]{2,1,0:T(8,128)(2,1)} %stack.2), calls=%async_computation | async-start | bytes 27262976 | tf_op jit(solution)/shard_map/all_to_all | solution.py:10
  23.2 195.9 %all-gather.2.cloned.1.call-start = ((), (), s32[]{:S(2)}) async-start(), calls=%async_computation.4 | async-start | bytes 2359296 | tf_op jit(solution)/shard_map/all_gather | solution.py:8
  23.9 247.5 %reduce-scatter.3.cloned.1.call-start = ((), (), s32[]{:S(2)}) async-start(), calls=%async_computation.3 | async-start | bytes 2359296 | tf_op jit(solution)/shard_map/reduce_scatter | solution.py:15
  219.0 182.9 %reduce-scatter.5.cloned.1.call-start = ((), (), s32[]{:S(2)}) async-start(), calls=%async_computation.5 | async-start | bytes 14483456 | tf_op jit(solution)/shard_map/reduce_scatter | solution.py:22
Sparse Core Ops, SparseCore 0:
  25.6 188.0 all-gather.1
  219.1 52.2 reduce-scatter.2
  276.4 125.4 reduce-scatter.4
